TPU v7x, 128 devices: a whole 4x4x4 slice. The times are simulated.
128 devices in a mesh: dp: 64 (over x, z_lo, y, core), tensor: 2 (over z_hi).
Axes of the slice: x: 4, y: 4, z: 4 (z_hi: 2, z_lo: 2; z = z_hi * 2 + z_lo), core: 2. Of those that a mesh axis runs over, the one named last changes fastest.
Arguments:
- tokens: bfloat16 [64, 512, 768], P('dp'), may hold values from -6 to 6
- counts: int32 [64], P('dp'), may hold values from 216 to 512, as said below
- ln1_gain: bfloat16 [768], replicated, may hold values from 0.5 to 1.5
- ln1_bias: bfloat16 [768], replicated, may hold values from -2 to 2
- qkv_weight: bfloat16 [768, 3, 768], P(None, None, 'tensor'), may hold values from -0.21875 to 0.21875
- qv_bias: bfloat16 [2, 768], P(None, 'tensor'), may hold values from -3 to 3
- out_weight: bfloat16 [768, 768], P('tensor'), may hold values from -3.5 to 3.5
- out_bias: bfloat16 [768], replicated, may hold values from -2 to 2
- ln2_gain: bfloat16 [768], replicated, may hold values from 0.5 to 1.5
- ln2_bias: bfloat16 [768], replicated, may hold values from -2 to 2
- up_weight: bfloat16 [768, 3072], P(None, 'tensor'), may hold values from -0.21875 to 0.21875
- up_bias: bfloat16 [3072], P('tensor'), may hold values from -3 to 3
- down_weight: bfloat16 [3072, 768], P('tensor'), may hold values from -0.21875 to 0.21875
- down_bias: bfloat16 [768], replicated, may hold values from -2 to 2
- cotangent: bfloat16 [64, 512, 768], P('dp'), may hold values from -6 to 6
Outputs:
- block_out: bfloat16 [64, 512, 768], P('dp')
- tokens_grad: bfloat16 [64, 512, 768], P('dp')
- ln1_gain_grad: float32 [768], replicated
- ln1_bias_grad: float32 [768], replicated
- qkv_weight_grad: float32 [768, 3, 768], P(None, None, 'tensor')
- qv_bias_grad: float32 [2, 768], P(None, 'tensor')
- out_weight_grad: float32 [768, 768], P('tensor')
- out_bias_grad: float32 [768], replicated
- ln2_gain_grad: float32 [768], replicated
- ln2_bias_grad: float32 [768], replicated
- up_weight_grad: float32 [768, 3072], P(None, 'tensor')
- up_bias_grad: float32 [3072], P('tensor')
- down_weight_grad: float32 [3072, 768], P('tensor')
- down_bias_grad: float32 [768], replicated
Inputs may be any that keep to these rules, and one draw needn't show every extreme that they name: `counts`: each item's real patches: 216, 256 or 512 (crops of 96^3, 64x128x128 and 128^3 voxels); the real patches come first.
All inputs are finite; a program needn't handle non-finite values.
Results may differ from a plain program's by a relative error of at most 0.012.
The roundings to bfloat16 on the way count: a program that leaves them out, or rounds other values in their place, can miss the bound.
Values sent between devices are 32-bit elements; how exact they have to be, the bound alone decides.
No kernel may reach another device: no remote copies, remote signals or barrier semaphores. Data moves between devices by JAX's collectives and lax.ppermute only.
A program may use at most 128 MiB of HBM per device.

v0:
```python
from functools import partial

import jax
import jax.numpy as jnp
from jax import lax
from jax.sharding import PartitionSpec as P

HEAD_DIM = 64


epsilon = 1e-06


def layer_norm(value, gain, shift):
    centre = value - jnp.mean(value, axis=-1, keepdims=True)
    spread = jnp.mean(centre * centre, axis=-1, keepdims=True)
    return centre * lax.rsqrt(spread + epsilon) * gain + shift


def left_trans(left, right):
    return lax.dot_general(
        left, right, (((0,), (0,)), ((), ())), preferred_element_type=jnp.float32
    )


def right_trans(left, right):
    return lax.dot_general(
        left, right, (((1,), (1,)), ((), ())), preferred_element_type=jnp.float32
    )


def attend_item(inputs):
    packed, valid_keys = inputs
    score_scale = HEAD_DIM ** (-0.5)
    query = packed[:, 0]
    key_part = packed[:, 1]
    value_part = packed[:, 2]
    scores = (
        jnp.einsum("qhd,khd->hqk", query, key_part, preferred_element_type=jnp.float32)
        * score_scale
    )
    scores = jnp.where(valid_keys[None, None, :], scores, -1000000000.0)
    largest = jnp.max(scores, axis=-1, keepdims=True)
    expo = jnp.exp(scores - largest)
    total = jnp.sum(expo, axis=-1, keepdims=True)
    probs = expo / total
    log_total = (largest + jnp.log(total))[..., 0]
    attended = jnp.einsum(
        "hqk,khd->qhd", probs.astype(jnp.bfloat16), value_part, preferred_element_type=jnp.float32
    )
    return (attended.astype(jnp.bfloat16), log_total)


def attend_back(inputs):
    packed, valid_keys, log_total, grad_att = inputs
    score_scale = HEAD_DIM ** (-0.5)
    query = packed[:, 0]
    key_part = packed[:, 1]
    value_part = packed[:, 2]
    scores = (
        jnp.einsum("qhd,khd->hqk", query, key_part, preferred_element_type=jnp.float32)
        * score_scale
    )
    scores = jnp.where(valid_keys[None, None, :], scores, -1000000000.0)
    probs = jnp.exp(scores - log_total[..., None])
    grad_value = jnp.einsum(
        "hqk,qhd->khd", probs.astype(jnp.bfloat16), grad_att, preferred_element_type=jnp.float32
    )
    grad_probs = jnp.einsum(
        "qhd,khd->hqk", grad_att, value_part, preferred_element_type=jnp.float32
    )
    grad_scores = probs * (grad_probs - jnp.sum(grad_probs * probs, axis=-1, keepdims=True))
    grad_low = grad_scores.astype(jnp.bfloat16)
    grad_query = (
        jnp.einsum("hqk,khd->qhd", grad_low, key_part, preferred_element_type=jnp.float32)
        * score_scale
    )
    grad_key = (
        jnp.einsum("hqk,qhd->khd", grad_low, query, preferred_element_type=jnp.float32)
        * score_scale
    )
    return jnp.stack([grad_query, grad_key, grad_value], axis=1)


def body(
    tokens,
    counts,
    ln1_gain,
    ln1_bias,
    qkv_weight,
    qv_bias,
    out_weight,
    out_bias,
    ln2_gain,
    ln2_bias,
    up_weight,
    up_bias,
    down_weight,
    down_bias,
    cotangent,
):
    items, patches, width = tokens.shape
    local_width = qkv_weight.shape[2]
    local_heads = local_width // HEAD_DIM
    rows = items * patches
    positions = jnp.arange(patches, dtype=jnp.int32)
    valid_keys = positions[None, :] < counts[:, None]
    row_valid = valid_keys.astype(jnp.float32).reshape(rows, 1)
    gain_one = ln1_gain.astype(jnp.float32)
    shift_one = ln1_bias.astype(jnp.float32)
    gain_two = ln2_gain.astype(jnp.float32)
    shift_two = ln2_bias.astype(jnp.float32)
    inputs = tokens.astype(jnp.float32).reshape(rows, width)
    normed, norm_one_back = jax.vjp(layer_norm, inputs, gain_one, shift_one)
    normed_low = normed.astype(jnp.bfloat16)
    flat_qkv = qkv_weight.reshape(width, 3 * local_width)
    bias_f = qv_bias.astype(jnp.float32)
    bias_rows = jnp.stack([bias_f[0], jnp.zeros((local_width,), jnp.float32), bias_f[1]])
    packed = (
        jnp.dot(normed_low, flat_qkv, preferred_element_type=jnp.float32).reshape(
            rows, 3, local_width
        )
        + bias_rows
    )
    packed_low = packed.astype(jnp.bfloat16).reshape(items, patches, 3, local_heads, HEAD_DIM)
    attended, log_total = lax.map(attend_item, (packed_low, valid_keys))
    attended_low = attended.reshape(rows, local_width)
    branch = lax.psum(
        jnp.dot(attended_low, out_weight, preferred_element_type=jnp.float32), "tensor"
    )
    middle = inputs + branch + out_bias.astype(jnp.float32)
    normed_two, norm_two_back = jax.vjp(layer_norm, middle, gain_two, shift_two)
    normed_two_low = normed_two.astype(jnp.bfloat16)
    upward = jnp.dot(
        normed_two_low, up_weight, preferred_element_type=jnp.float32
    ) + up_bias.astype(jnp.float32)
    activated, gelu_back = jax.vjp(partial(jax.nn.gelu, approximate=False), upward)
    activated_low = activated.astype(jnp.bfloat16)
    downward = lax.psum(
        jnp.dot(activated_low, down_weight, preferred_element_type=jnp.float32), "tensor"
    )
    block_out = ((middle + downward + down_bias.astype(jnp.float32)) * row_valid).astype(
        jnp.bfloat16
    )
    grad_out = cotangent.astype(jnp.float32).reshape(rows, width) * row_valid
    down_bias_grad = jnp.sum(grad_out, axis=0)
    grad_down = grad_out.astype(jnp.bfloat16)
    down_weight_grad = left_trans(activated_low, grad_down)
    grad_act = right_trans(grad_down, down_weight)
    grad_up = gelu_back(grad_act)[0].astype(jnp.bfloat16)
    up_bias_grad = jnp.sum(grad_up.astype(jnp.float32), axis=0)
    up_weight_grad = left_trans(normed_two_low, grad_up)
    grad_normed_two = lax.psum(right_trans(grad_up, up_weight), "tensor")
    grad_mid_norm, ln2_gain_grad, ln2_bias_grad = norm_two_back(grad_normed_two)
    grad_middle = grad_out + grad_mid_norm
    out_bias_grad = jnp.sum(grad_middle, axis=0)
    grad_branch = grad_middle.astype(jnp.bfloat16)
    out_weight_grad = left_trans(attended_low, grad_branch)
    grad_attended = (
        right_trans(grad_branch, out_weight)
        .astype(jnp.bfloat16)
        .reshape(items, patches, local_heads, HEAD_DIM)
    )
    grad_packed = lax.map(attend_back, (packed_low, valid_keys, log_total, grad_attended))
    grad_packed_low = grad_packed.astype(jnp.bfloat16).reshape(rows, 3 * local_width)
    grad_sums_cols = jnp.sum(grad_packed_low.astype(jnp.float32), axis=0).reshape(3, local_width)
    qv_bias_grad = jnp.stack([grad_sums_cols[0], grad_sums_cols[2]])
    qkv_weight_grad = left_trans(normed_low, grad_packed_low).reshape(width, 3, local_width)
    grad_normed = lax.psum(right_trans(grad_packed_low, flat_qkv), "tensor")
    grad_in_norm, ln1_gain_grad, ln1_bias_grad = norm_one_back(grad_normed)
    tokens_grad = (grad_middle + grad_in_norm).astype(jnp.bfloat16).reshape(items, patches, width)
    (
        ln1_gain_grad,
        ln1_bias_grad,
        qkv_weight_grad,
        qv_bias_grad,
        out_weight_grad,
        out_bias_grad,
        ln2_gain_grad,
        ln2_bias_grad,
        up_weight_grad,
        up_bias_grad,
        down_weight_grad,
        down_bias_grad,
    ) = lax.psum(
        (
            ln1_gain_grad,
            ln1_bias_grad,
            qkv_weight_grad,
            qv_bias_grad,
            out_weight_grad,
            out_bias_grad,
            ln2_gain_grad,
            ln2_bias_grad,
            up_weight_grad,
            up_bias_grad,
            down_weight_grad,
            down_bias_grad,
        ),
        "dp",
    )
    return (
        block_out.reshape(items, patches, width),
        tokens_grad,
        ln1_gain_grad,
        ln1_bias_grad,
        qkv_weight_grad,
        qv_bias_grad,
        out_weight_grad,
        out_bias_grad,
        ln2_gain_grad,
        ln2_bias_grad,
        up_weight_grad,
        up_bias_grad,
        down_weight_grad,
        down_bias_grad,
    )


def solution(mesh):
    in_specs = (
        P("dp", None, None),
        P("dp"),
        P(),
        P(),
        P(None, None, "tensor"),
        P(None, "tensor"),
        P("tensor", None),
        P(),
        P(),
        P(),
        P(None, "tensor"),
        P("tensor"),
        P("tensor", None),
        P(),
        P("dp", None, None),
    )
    out_specs = (
        P("dp", None, None),
        P("dp", None, None),
        P(),
        P(),
        P(None, None, "tensor"),
        P(None, "tensor"),
        P("tensor", None),
        P(),
        P(),
        P(),
        P(None, "tensor"),
        P("tensor"),
        P("tensor", None),
        P(),
    )
    return jax.shard_map(body, mesh=mesh, in_specs=in_specs, out_specs=out_specs, check_vma=False)
```

profile of v0, /device:TPU:1, one launch (start us, length us, event | category | flops | bytes accessed | tf_op | source)
XLA Modules:
  0.0 892.1 jit_solution(15157510432403861540)
XLA Ops:
  8.1 3.9 copy.34
  13.3 2.8 add_convert_fusion.1
  16.1 1.5 fusion.71
  17.6 0.9 fusion
  18.5 1.7 copy-done.2
  20.3 1.2 fusion.39
  21.5 1.7 fusion.72
  23.5 0.6 convert_element_type.143
  24.1 0.7 convert_element_type.141
  24.8 0.7 convert_element_type.140
  25.5 60.8 %all-reduce.8.cloned.1.call-done = f32[512,768]{1,0:T(8,128)} async-done(((f32[512,768]{1,0:T(8,128)}), f32[512,768]{1,0:T(8,128)}) %all-reduce.8.cloned.1.call-update) | async-done | bytes 1572880 | tf_op jit(solution)/shard_map/psum | solution.py:128
  86.3 1.7 fusion.67
  88.3 0.8 copy-done.48
  89.2 9.0 %multiply_convert_fusion.1 = (bf16[512,1536]{1,0:T(8,128)(2,1)}, f32[512,1536]{1,0:T(8,128)S(1)}, f32[512,1536]{1,0:T(8,128)S(1)}) fusion(f32[1536]{0:T(1024)S(1)} %copy-done.55, bf16[768,1536]{1,0:T(8,128)(2,1)S(1)} %copy-done, f32[512,768]{1,0:T(8,128)S(1)} %get-tuple-element.77, f32[768]{0:T(1024)S(1)} %convert_element_type.141, ...), kind=kOutput, calls=%fused_computation.15 | convolution fusion | flops 1261830144 | bytes 11812864 | tf_op jit(solution)/shard_map/dot_general | solution.py:134
  98.2 2.9 convert_reduce_fusion
  101.1 1.1 copy-done.68
  102.3 2.6 fusion.74
  105.6 4.8 fusion.73
  110.4 53.4 %all-reduce.10.cloned.1.call-done = f32[512,768]{1,0:T(8,128)} async-done(((f32[512,768]{1,0:T(8,128)}), f32[512,768]{1,0:T(8,128)}) %all-reduce.10.cloned.1.call-update) | async-done | bytes 1572880 | tf_op jit(solution)/shard_map/psum | solution.py:153
  163.9 2.8 multiply_reduce_fusion.1
  166.8 0.6 fusion.65
  167.5 0.7 convolution_convert_fusion
  168.5 5.3 fusion.34
  173.8 2.4 multiply_reduce_fusion
  176.2 1.9 multiply_convert_fusion
  178.1 2.1 fusion.37
  180.1 1.7 fusion.38
  181.8 0.8 convert_reduce_fusion.2
  182.7 1.0 copy-done.15
  183.7 2.4 fusion.75
  186.8 5.2 fusion.47
  192.0 4.1 fusion.60
  196.2 1.8 fusion.43
  198.0 3.3 fusion.56
  201.3 0.7 copy-done.66
  202.2 77.4 %all-reduce.14.cloned.1.call-done = (f32[512,768]{1,0:T(8,128)}, f32[512,768]{1,0:T(8,128)}) async-done(((f32[512,768]{1,0:T(8,128)}, f32[512,768]{1,0:T(8,128)}), (f32[512,768]{1,0:T(8,128)}, f32[512,768]{1,0:T(8,128)})) %all-reduce.14.cloned.1.call-update) | async-done | bytes 3145744 | tf_op jit(solution)/shard_map/psum | solution.py:139
  279.6 2.0 fusion.64
  281.7 0.8 fusion.23
  282.5 0.6 copy-done.9
  283.1 2.1 fusion.29
  285.3 273.6 %all-reduce = (f32[768]{0:T(1024)}, f32[768]{0:T(1024)}, f32[2,384]{1,0:T(2,128)}, f32[768]{0:T(1024)}, f32[768]{0:T(1024)}, /*index=5*/f32[768]{0:T(1024)}, f32[1536]{0:T(1024)}, f32[768]{0:T(1024)}) all-reduce(f32[768]{0:T(1024)S(1)} %get-tuple-element.49, ...), channel_id=1, replica_groups=mesh['dp'=64,'tensor'=2] {'dp'}, use_global_device_ids=true, to_apply=%region_16.17 | all-reduce | flops 6912 | bytes 55296 | tf_op jit(solution)/shard_map/psum | solution.py:185
  558.8 314.8 %all-reduce.12.cloned.1.call-done = (f32[768,3,384]{2,0,1:T(8,128)}, f32[384,768]{1,0:T(8,128)}, f32[768,1536]{1,0:T(8,128)}, f32[1536,768]{1,0:T(8,128)}) async-done(((f32[768,3,384]{2,0,1:T(8,128)}, f32[384,768]{1,0:T(8,128)}, f32[768,1536]{1,0:T(8,128)}, f32[1536,768]{1,0:T(8,128)}), (f32[768,3,384]{2,0,1:T(8,128)}, f32[384,768]{1,0:T(8,128)}, f32[768,1536]{1,0:T(8,128)}, ...) | async-done | bytes 14155792 | tf_op jit(solution)/shard_map/psum | solution.py:185
  873.6 4.2 copy.55
  877.8 1.0 copy.56
  878.8 2.4 copy.57
  881.2 0.8 slice-done.2
  882.2 2.4 copy.58
  884.6 1.0 copy-done.1
  (175 shorter events, 4.3 us)
Async XLA Ops:
  7.2 81.9 %copy-start = (bf16[768,1536]{1,0:T(8,128)(2,1)S(1)}, bf16[768,1536]{1,0:T(8,128)(2,1)}, u32[]{:S(2)}) copy-start(bf16[768,1536]{1,0:T(8,128)(2,1)} %param.25) | copy-start | bytes 7077892
  7.2 79.1 %all-reduce.8.cloned.1.call-start = ((), (), s32[]{:S(2)}) async-start(), calls=%async_computation | async-start | bytes 3145728 | tf_op jit(solution)/shard_map/psum | solution.py:128
  8.0 4.0 copy-start.57
  8.0 4.0 copy-start.63
  8.1 4.0 copy-start.64
  8.1 4.0 copy-start.5
  12.0 4.0 copy-start.59
  12.1 4.0 copy-start.25
  12.3 3.8 copy-start.29
  12.7 3.4 copy-start.41
  17.6 2.6 copy-start.2
  17.6 2.7 copy-start.23
  21.5 2.6 copy-start.65
  23.3 140.6 %all-reduce.10.cloned.1.call-start = ((), (), s32[]{:S(2)}) async-start(), calls=%async_computation.1 | async-start | bytes 3145728 | tf_op jit(solution)/shard_map/psum | solution.py:153
  24.8 64.3 %copy-start.61 = (f32[768]{0:T(1024)}, f32[768]{0:T(1024)S(1)}, u32[]{:S(2)}) copy-start(f32[768]{0:T(1024)S(1)} %convert_element_type.141) | copy-start | bytes 9220
  25.5 63.6 %copy-start.31 = (f32[768]{0:T(1024)}, f32[768]{0:T(1024)S(1)}, u32[]{:S(2)}) copy-start(f32[768]{0:T(1024)S(1)} %convert_element_type.140) | copy-start | bytes 9220
  25.5 72.7 %copy-start.35 = (f32[512]{0:T(512)}, f32[512]{0:T(512)S(1)}, u32[]{:S(2)}) copy-start(f32[512]{0:T(512)S(1)} %fusion.55) | copy-start | bytes 6148
  88.0 10.2 %copy-start.3 = (f32[512,768]{1,0:T(8,128)}, f32[512,768]{1,0:T(8,128)S(1)}, u32[]{:S(2)}) copy-start(f32[512,768]{1,0:T(8,128)S(1)} %get-tuple-element.77) | copy-start | bytes 4718596
  88.0 10.2 %copy-start.38 = (f32[512]{0:T(512)}, f32[512]{0:T(512)S(1)}, u32[]{:S(2)}) copy-start(f32[512]{0:T(512)S(1)} %broadcast_multiply_fusion) | copy-start | bytes 6148
  89.1 9.0 %copy-start.50 = (f32[512]{0:T(512)}, f32[512]{0:T(512)S(1)}, u32[]{:S(2)}) copy-start(f32[512]{0:T(512)S(1)} %fusion.54) | copy-start | bytes 6148
  89.1 9.0 %copy-start.11 = (bf16[1,512,768]{2,1,0:T(8,128)(2,1)S(1)}, bf16[1,512,768]{2,1,0:T(8,128)(2,1)}, u32[]{:S(2)}) copy-start(bf16[1,512,768]{2,1,0:T(8,128)(2,1)} %param.29) | copy-start | bytes 2359300
  89.2 9.0 %copy-start.67 = (bf16[1536,768]{1,0:T(8,128)(2,1)S(1)}, bf16[1536,768]{1,0:T(8,128)(2,1)}, u32[]{:S(2)}) copy-start(bf16[1536,768]{1,0:T(8,128)(2,1)} %param.27) | copy-start | bytes 7077892
  104.9 174.7 %all-reduce.14.cloned.1.call-start = ((), (), s32[]{:S(2)}) async-start(), calls=%async_computation.3 | async-start | bytes 6291456 | tf_op jit(solution)/shard_map/psum | solution.py:139
  105.6 58.3 %copy-start.4 = (f32[512,768]{1,0:T(8,128)S(1)}, f32[512,768]{1,0:T(8,128)}, u32[]{:S(2)}) copy-start(f32[512,768]{1,0:T(8,128)} %copy-done.3) | copy-start | bytes 4718596
  163.9 2.8 copy-start.49
  163.9 2.8 copy-start.13
  163.9 2.8 copy-start.32
  163.9 2.8 copy-start.39
  163.9 2.8 copy-start.51
  163.9 3.5 copy-start.12
  163.9 3.5 copy-start.22
  166.8 7.1 slice-start
  167.5 6.4 slice-start.1
  186.1 5.9 copy-start.33
  186.1 5.9 copy-start.40
  186.1 5.8 copy-start.52
  186.2 687.5 %all-reduce.12.cloned.1.call-start = ((), (), s32[]{:S(2)}) async-start(), calls=%async_computation.2 | async-start | bytes 28311552 | tf_op jit(solution)/shard_map/psum | solution.py:185
  186.8 5.2 copy-start.62
  186.8 5.2 copy-start.69
  192.0 4.1 copy-start.8
  192.0 4.1 copy-start.44
  202.0 79.6 %copy-start.47 = (f32[512]{0:T(512)S(1)}, f32[512]{0:T(512)}, u32[]{:S(2)}) copy-start(f32[512]{0:T(512)} %copy-done.46) | copy-start | bytes 6148
  279.6 2.9 copy-start.18
  873.6 4.2 copy-start.20
  873.6 5.2 copy-start.14
  877.8 4.2 slice-start.2
  878.8 3.4 slice-start.3
  882.2 3.4 copy-start.1
  (30 other events, 42.3 us)
Sparse Core Ops, SparseCore 0:
  23.4 62.8 all-reduce.7
  105.0 58.8 all-reduce.9
  186.2 93.3 all-reduce.13
  283.6 589.9 all-reduce.11
where the time goes:
time: 893 us; the launch traced here: 892 us
  waiting for transfers between devices  506 us (57%)
  blocking collectives  274 us (31%)
  matrix products  55.4 us (6%)
  local copies, waits for them, and re-layouts  24 us (3%)
  other arithmetic  16.6 us (2%)
  between operations  15.3 us (2%)
    psum x1, waiting for transfers between devices, body(): lax.psum((ln1_gain_grad, ln1_bias_grad, qkv_weight_grad, qv_bias_grad, ou...  315 us
    psum x1, blocking collectives, body(): lax.psum((ln1_gain_grad, ln1_bias_grad, qkv_weight_grad, qv_bias_grad, ou...  274 us
    psum x1, waiting for transfers between devices, body(): lax.psum(jnp.dot(activated_low, down_weight, preferred_element_type=jnp.f...  77.4 us
    psum x1, waiting for transfers between devices, body(): lax.psum(jnp.dot(attended_low, out_weight, preferred_element_type=jnp.flo...  60.8 us
    psum x1, waiting for transfers between devices, body(): grad_normed_two = lax.psum(right_trans(grad_up, up_weight), 'tensor')  53.4 us
    unnamed x153, local copies, waits for them, and re-layouts  23.7 us
  transfers between devices with their start and end apart: 4, of which 4 were waited for; matrix products, arithmetic and copies ran while one was open for 3% of the time, Pallas kernels for 0%

commit v1 on v0

--- a/solution.py
+++ b/solution.py
@@ -2,13 +2,87 @@
 
 import jax
 import jax.numpy as jnp
+import numpy as np
 from jax import lax
 from jax.sharding import PartitionSpec as P
 
 HEAD_DIM = 64
+RING = 4
+DP_SHAPE = (4, 2, 4, 2)
 
 
 epsilon = 1e-06
+
+
+def dp_moves(move):
+    pairs = []
+    for source in range(int(np.prod(DP_SHAPE))):
+        where = [int(v) for v in np.unravel_index(source, DP_SHAPE)]
+        pairs.append((source, int(np.ravel_multi_index(move(*where), DP_SHAPE))))
+    return pairs
+
+
+CORE_SWAP = dp_moves(lambda x, z, y, c: (x, z, y, 1 - c))
+Z_SWAP = dp_moves(lambda x, z, y, c: (x, 1 - z, y, c))
+
+
+def first_shift(k):
+    return dp_moves(
+        lambda x, z, y, c: ((x + k) % RING, z, y, c) if c == 0 else (x, z, (y + k) % RING, c)
+    )
+
+
+def second_shift(k):
+    return dp_moves(
+        lambda x, z, y, c: (x, z, (y + k) % RING, c) if c == 0 else ((x + k) % RING, z, y, c)
+    )
+
+
+def places():
+    at = lax.axis_index("dp")
+    core = at % 2
+    y = (at // 2) % RING
+    x = at // 16
+    return core, jnp.where(core == 0, x, y), jnp.where(core == 0, y, x)
+
+
+def pick(blocks, at):
+    return lax.dynamic_index_in_dim(blocks, at, 0, keepdims=False)
+
+
+def scatter_ring(blocks, at, shift):
+    arrived = [
+        lax.ppermute(pick(blocks, (at + k) % RING), "dp", shift(k)) for k in range(1, RING)
+    ]
+    return pick(blocks, at) + arrived[0] + arrived[1] + arrived[2]
+
+
+def gather_ring(block, at, shift):
+    whole = jnp.zeros((RING,) + block.shape, block.dtype)
+    whole = lax.dynamic_update_index_in_dim(whole, block, at, 0)
+    for k in range(1, RING):
+        arrived = lax.ppermute(block, "dp", shift(k))
+        whole = lax.dynamic_update_index_in_dim(whole, arrived, (at - k) % RING, 0)
+    return whole
+
+
+def sum_items(halves):
+    core, first, second = places()
+    rows, columns = halves.shape[1:]
+    mine = pick(halves, core) + lax.ppermute(pick(halves, 1 - core), "dp", CORE_SWAP)
+    mine = scatter_ring(mine.reshape(RING, rows // 4, columns), first, first_shift)
+    mine = scatter_ring(mine.reshape(RING, rows // 16, columns), second, second_shift)
+    mine = mine + lax.ppermute(mine, "dp", Z_SWAP)
+    mine = gather_ring(mine, second, second_shift).reshape(rows // 4, columns)
+    mine = gather_ring(mine, first, first_shift).reshape(rows, columns)
+    other = lax.ppermute(mine, "dp", CORE_SWAP)
+    whole = jnp.zeros_like(halves)
+    whole = lax.dynamic_update_index_in_dim(whole, mine, core, 0)
+    return lax.dynamic_update_index_in_dim(whole, other, 1 - core, 0)
+
+
+def sum_pair(value):
+    return value + lax.ppermute(value, "tensor", [(0, 1), (1, 0)])
 
 
 def layer_norm(value, gain, shift):
@@ -102,6 +176,7 @@
     items, patches, width = tokens.shape
     local_width = qkv_weight.shape[2]
     local_heads = local_width // HEAD_DIM
+    hidden = up_weight.shape[1]
     rows = items * patches
     positions = jnp.arange(patches, dtype=jnp.int32)
     valid_keys = positions[None, :] < counts[:, None]
@@ -125,9 +200,7 @@
     packed_low = packed.astype(jnp.bfloat16).reshape(items, patches, 3, local_heads, HEAD_DIM)
     attended, log_total = lax.map(attend_item, (packed_low, valid_keys))
     attended_low = attended.reshape(rows, local_width)
-    branch = lax.psum(
-        jnp.dot(attended_low, out_weight, preferred_element_type=jnp.float32), "tensor"
-    )
+    branch = sum_pair(jnp.dot(attended_low, out_weight, preferred_element_type=jnp.float32))
     middle = inputs + branch + out_bias.astype(jnp.float32)
     normed_two, norm_two_back = jax.vjp(layer_norm, middle, gain_two, shift_two)
     normed_two_low = normed_two.astype(jnp.bfloat16)
@@ -136,21 +209,25 @@
     ) + up_bias.astype(jnp.float32)
     activated, gelu_back = jax.vjp(partial(jax.nn.gelu, approximate=False), upward)
     activated_low = activated.astype(jnp.bfloat16)
-    downward = lax.psum(
-        jnp.dot(activated_low, down_weight, preferred_element_type=jnp.float32), "tensor"
-    )
-    block_out = ((middle + downward + down_bias.astype(jnp.float32)) * row_valid).astype(
-        jnp.bfloat16
-    )
     grad_out = cotangent.astype(jnp.float32).reshape(rows, width) * row_valid
     down_bias_grad = jnp.sum(grad_out, axis=0)
     grad_down = grad_out.astype(jnp.bfloat16)
-    down_weight_grad = left_trans(activated_low, grad_down)
     grad_act = right_trans(grad_down, down_weight)
     grad_up = gelu_back(grad_act)[0].astype(jnp.bfloat16)
+    grad_normed_two = sum_pair(right_trans(grad_up, up_weight))
+    downward = sum_pair(jnp.dot(activated_low, down_weight, preferred_element_type=jnp.float32))
+    block_out = ((middle + downward + down_bias.astype(jnp.float32)) * row_valid).astype(
+        jnp.bfloat16
+    )
+    down_weight_grad = left_trans(activated_low, grad_down).reshape(2, hidden // 2, width)
     up_bias_grad = jnp.sum(grad_up.astype(jnp.float32), axis=0)
-    up_weight_grad = left_trans(normed_two_low, grad_up)
-    grad_normed_two = lax.psum(right_trans(grad_up, up_weight), "tensor")
+    up_weight_grad = jnp.stack(
+        [
+            left_trans(normed_two_low, grad_up[:, : hidden // 2]),
+            left_trans(normed_two_low, grad_up[:, hidden // 2 :]),
+        ]
+    )
+    hidden_sums = sum_items(jnp.concatenate([down_weight_grad, up_weight_grad], axis=1))
     grad_mid_norm, ln2_gain_grad, ln2_bias_grad = norm_two_back(grad_normed_two)
     grad_middle = grad_out + grad_mid_norm
     out_bias_grad = jnp.sum(grad_middle, axis=0)
@@ -165,15 +242,79 @@
     grad_packed_low = grad_packed.astype(jnp.bfloat16).reshape(rows, 3 * local_width)
     grad_sums_cols = jnp.sum(grad_packed_low.astype(jnp.float32), axis=0).reshape(3, local_width)
     qv_bias_grad = jnp.stack([grad_sums_cols[0], grad_sums_cols[2]])
-    qkv_weight_grad = left_trans(normed_low, grad_packed_low).reshape(width, 3, local_width)
-    grad_normed = lax.psum(right_trans(grad_packed_low, flat_qkv), "tensor")
+    qkv_weight_grad = left_trans(normed_low, grad_packed_low)
+    grad_normed = sum_pair(right_trans(grad_packed_low, flat_qkv))
     grad_in_norm, ln1_gain_grad, ln1_bias_grad = norm_one_back(grad_normed)
     tokens_grad = (grad_middle + grad_in_norm).astype(jnp.bfloat16).reshape(items, patches, width)
+
+    half = width // 2
+    small = jnp.concatenate(
+        [
+            ln1_gain_grad,
+            ln1_bias_grad,
+            qv_bias_grad.reshape(-1),
+            out_bias_grad,
+            ln2_gain_grad,
+            ln2_bias_grad,
+            up_bias_grad,
+            down_bias_grad,
+        ]
+    )
+    small_rows = small.shape[0] // local_width
+    small = small.reshape(2, small_rows // 2, local_width)
+    spare = (-small.shape[1]) % 128
+    qkv_halves = (
+        qkv_weight_grad.reshape(2, half, 3, local_width)
+        .transpose(0, 2, 1, 3)
+        .reshape(2, 3 * half, local_width)
+    )
+    out_halves = (
+        out_weight_grad.reshape(2, local_width // 2, 2, half)
+        .transpose(0, 2, 1, 3)
+        .reshape(2, local_width, half)
+    )
+    late_sums = sum_items(
+        jnp.concatenate(
+            [qkv_halves, out_halves, small, jnp.zeros((2, spare, local_width), jnp.float32)], axis=1
+        )
+    )
+    qkv_end = 3 * half
+    out_end = qkv_end + local_width
+    qkv_weight_grad = (
+        late_sums[:, :qkv_end]
+        .reshape(2, 3, half, local_width)
+        .transpose(0, 2, 1, 3)
+        .reshape(width, 3, local_width)
+    )
+    out_weight_grad = (
+        late_sums[:, qkv_end:out_end]
+        .reshape(2, 2, local_width // 2, half)
+        .transpose(0, 2, 1, 3)
+        .reshape(local_width, width)
+    )
+    small = late_sums[:, out_end : out_end + small_rows // 2].reshape(-1)
+    ends = np.cumsum([width, width, 2 * local_width, width, width, width, hidden, width])
     (
         ln1_gain_grad,
         ln1_bias_grad,
+        qv_bias_grad,
+        out_bias_grad,
+        ln2_gain_grad,
+        ln2_bias_grad,
+        up_bias_grad,
+        down_bias_grad,
+    ) = jnp.split(small, ends[:-1])
+    down_weight_grad = hidden_sums[:, : hidden // 2].reshape(hidden, width)
+    up_weight_grad = jnp.concatenate(
+        [hidden_sums[0, hidden // 2 :], hidden_sums[1, hidden // 2 :]], axis=1
+    )
+    return (
+        block_out.reshape(items, patches, width),
+        tokens_grad,
+        ln1_gain_grad,
+        ln1_bias_grad,
         qkv_weight_grad,
-        qv_bias_grad,
+        qv_bias_grad.reshape(2, local_width),
         out_weight_grad,
         out_bias_grad,
         ln2_gain_grad,
@@ -182,38 +323,6 @@
         up_bias_grad,
         down_weight_grad,
         down_bias_grad,
-    ) = lax.psum(
-        (
-            ln1_gain_grad,
-            ln1_bias_grad,
-            qkv_weight_grad,
-            qv_bias_grad,
-            out_weight_grad,
-            out_bias_grad,
-            ln2_gain_grad,
-            ln2_bias_grad,
-            up_weight_grad,
-            up_bias_grad,
-            down_weight_grad,
-            down_bias_grad,
-        ),
-        "dp",
-    )
-    return (
-        block_out.reshape(items, patches, width),
-        tokens_grad,
-        ln1_gain_grad,
-        ln1_bias_grad,
-        qkv_weight_grad,
-        qv_bias_grad,
-        out_weight_grad,
-        out_bias_grad,
-        ln2_gain_grad,
-        ln2_bias_grad,
-        up_weight_grad,
-        up_bias_grad,
-        down_weight_grad,
-        down_bias_grad,
     )
 
 

time: 893 us -> 435 us (0.49)
  waiting for transfers between devices: 506 us -> 194 us
  blocking collectives: 274 us -> 0 us
  local copies, waits for them, and re-layouts: 24 us -> 85.9 us
  starting transfers between devices: 0.83 us -> 43.2 us
  other arithmetic: 16.6 us -> 57.7 us
  between operations: 15.3 us -> 2.68 us
  matrix products: 55.4 us -> 45.1 us
    psum x4 -> x0, waiting for transfers between devices: 506 us -> none  [the longest x1 315 us: body(): lax.psum((ln1_gain_grad, ln1_bias_grad, qkv_weight_grad, qv_bias_grad, ou...]
    psum x1 -> x0, blocking collectives: 274 us -> none  [body(): lax.psum((ln1_gain_grad, ln1_bias_grad, qkv_weight_grad, qv_bias_grad, ou...]
    ppermute x0 -> x34, waiting for transfers between devices: none -> 194 us  [the longest x4 102 us: sum_pair(): return value + lax.ppermute(value, 'tensor', [(0, 1), (1, 0)])]
    ppermute x0 -> x34, starting transfers between devices: none -> 43.2 us  [the longest x12 13.4 us: gather_ring(): arrived = lax.ppermute(block, 'dp', shift(k))]
    dynamic_update_slice x0 -> x18, local copies, waits for them, and re-layouts: none -> 16.1 us  [the longest x2 5.08 us: sum_items(): whole = lax.dynamic_update_index_in_dim(whole, mine, core, 0)]
    concatenate x0 -> x2, local copies, waits for them, and re-layouts: none -> 13.5 us  [the longest x1 13.5 us: body(): jnp.concatenate([qkv_halves, out_halves, small, jnp.zeros((2, spare, loca...]
    squeeze x0 -> x7, local copies, waits for them, and re-layouts: none -> 12.8 us  [the longest x6 10.1 us: pick(): return lax.dynamic_index_in_dim(blocks, at, 0, keepdims=False)]
    add x0 -> x6, other arithmetic: none -> 11.5 us  [the longest x2 6.36 us: sum_items(): pick(halves, core) + lax.ppermute(pick(halves, 1 - core), 'dp', CORE_SWAP)]
  transfers between devices with their start and end apart: 4 -> 34, of which waited for: 4 -> 17; matrix products, arithmetic and copies ran while one was open for 3% -> 25% of each run, Pallas kernels for 0% -> 0%
where the time goes in v1:
time: 435 us; the launch traced here: 429 us
  waiting for transfers between devices  194 us (45%)
  local copies, waits for them, and re-layouts  85.9 us (20%)
  other arithmetic  57.7 us (13%)
  matrix products  45.1 us (10%)
  starting transfers between devices  43.2 us (10%)
    ppermute x4, waiting for transfers between devices, sum_pair(): return value + lax.ppermute(value, 'tensor', [(0, 1), (1, 0)])  102 us
    ppermute x12, waiting for transfers between devices, scatter_ring(): lax.ppermute(pick(blocks, (at + k) % RING), 'dp', shift(k))  48.1 us
    ppermute x12, waiting for transfers between devices, gather_ring(): arrived = lax.ppermute(block, 'dp', shift(k))  41.2 us
    unnamed x163, local copies, waits for them, and re-layouts  15 us
    concatenate x1, local copies, waits for them, and re-layouts, body(): jnp.concatenate([qkv_halves, out_halves, small, jnp.zeros((2, spare, loca...  13.5 us
    ppermute x12, starting transfers between devices, gather_ring(): arrived = lax.ppermute(block, 'dp', shift(k))  13.4 us
    dot_general x5, matrix products, left_trans(): lax.dot_general(left, right, (((0,), (0,)), ((), ())), preferred_element_...  12.4 us
    squeeze x6, local copies, waits for them, and re-layouts, pick(): return lax.dynamic_index_in_dim(blocks, at, 0, keepdims=False)  10.1 us
  transfers between devices with their start and end apart: 34, of which 17 were waited for; matrix products, arithmetic and copies ran while one was open for 25% of the time, Pallas kernels for 0%

profile of v1, /device:TPU:1, one launch (start us, length us, event | category | flops | bytes accessed | tf_op | source)
XLA Modules:
  0.0 428.8 jit_solution(3831739953447643510)
XLA Ops:
  0.7 4.0 copy.46
  6.2 2.8 add_convert_fusion.1
  16.2 4.6 %collective-permute-start = (f32[512,768]{1,0:T(8,128)}, f32[512,768]{1,0:T(8,128)}, u32[]{:S(2)}, u32[]{:S(2)}) collective-permute-start(f32[512,768]{1,0:T(8,128)} %fusion.109), channel_id=1, source_target_pairs={{0,1},{1,0},{2,3},{3,2},{4,5},{5,4},{6,7},{7,6},{8,9},{9,8},{10,11... | collective-permute-start | bytes 4718600 | tf_op jit(solution)/shard_map/ppermute | solution.py:85
  25.2 30.0 %collective-permute-done = f32[512,768]{1,0:T(8,128)} collective-permute-done((f32[512,768]{1,0:T(8,128)}, f32[512,768]{1,0:T(8,128)}, u32[]{:S(2)}, u32[]{:S(2)}) %collective-permute-start) | collective-permute-done | bytes 1572896 | tf_op jit(solution)/shard_map/ppermute | solution.py:85
  58.6 7.6 %fusion.2 = (f32[512,1536]{1,0:T(8,128)S(1)}, f32[512,1536]{1,0:T(8,128)S(1)}) fusion(f32[1536]{0:T(1024)S(1)} %copy-done.58, bf16[768,1536]{1,0:T(8,128)(2,1)S(1)} %copy-done, f32[512,768]{1,0:T(8,128)S(1)} %get-tuple-element.67, f32[768]{0:T(1024)S(1)} %copy-done.64, f32[768]{0:T(1024)S(1)} %copy-done.32, f32[512]{0:T(512)S(1)} %fusion.95, ...), kind=kOutput, calls=%fused_computation.17 | convolution fusion | flops 1259470848 | bytes 10240000 | tf_op jit(solution)/shard_map/dot_general | solution.py:207
  66.2 7.7 %fusion.5 = bf16[1536,512]{0,1:T(8,128)(2,1)} fusion(f32[512,1536]{1,0:T(8,128)S(1)} %get-tuple-element.99), kind=kLoop, calls=%fused_computation.20 | loop fusion | flops 51118080 | bytes 4718592 | tf_op jit(solution)/shard_map/convert_element_type | solution.py:211
  73.9 2.9 convert_reduce_fusion
  76.8 2.6 fusion.110
  79.4 2.6 collective-permute-start.2
  82.0 2.6 fusion.54
  91.8 2.9 fusion.71
  94.8 6.8 %maximum_maximum_fusion = f32[2,1536,768]{2,1,0:T(8,128)} fusion(f32[1,768,768]{2,1,0:T(8,128)} %convolution_bitcast_fusion, f32[1,768,768]{2,1,0:T(8,128)} %convolution_bitcast_fusion.1, f32[2,768,768]{2,1,0:T(8,128)S(1)} %fusion.71), kind=kLoop, calls=%fused_computation | loop fusion | flops 4718592 | bytes 18874368 | tf_op jit(solution)/shard_map/concatenate | solution.py:230
  101.6 14.3 %collective-permute-done.2 = f32[512,768]{1,0:T(8,128)} collective-permute-done((f32[512,768]{1,0:T(8,128)}, f32[512,768]{1,0:T(8,128)}, u32[]{:S(2)}, u32[]{:S(2)}) %collective-permute-start.2) | collective-permute-done | bytes 1572896 | tf_op jit(solution)/shard_map/ppermute | solution.py:85
  115.9 3.2 multiply_reduce_fusion.1
  119.1 30.5 %collective-permute-done.1 = f32[512,768]{1,0:T(8,128)} collective-permute-done((f32[512,768]{1,0:T(8,128)}, f32[512,768]{1,0:T(8,128)}, u32[]{:S(2)}, u32[]{:S(2)}) %collective-permute-start.1) | collective-permute-done | bytes 1572896 | tf_op jit(solution)/shard_map/ppermute | solution.py:85
  149.6 3.8 fusion.102
  155.4 4.0 multiply_reduce_fusion
  159.4 4.7 %multiply_convert_fusion = bf16[6,512,512]{1,2,0:T(8,128)(2,1)S(1)} fusion(f32[6,512,512]{1,2,0:T(8,128)} %get-tuple-element.101, f32[6,512,512]{1,2,0:T(8,128)S(1)} %bitcast.363, f32[6,512]{1,0:T(8,128)S(1)} %get-tuple-element.100, f32[6,512]{1,0:T(8,128)S(1)} %log_add_fusion), kind=kLoop, calls=%fused_computation.1 | loop fusion | flops 6291456 | bytes 15753216 | tf_op jit(solution)/shard_map/while/body/eval_jaxpr/convert_element_type | solution.py:147
  173.9 2.9 collective-permute-start.19
  177.6 27.0 %collective-permute-done.3 = f32[512,768]{1,0:T(8,128)} collective-permute-done((f32[512,768]{1,0:T(8,128)}, f32[512,768]{1,0:T(8,128)}, u32[]{:S(2)}, u32[]{:S(2)}) %collective-permute-start.3) | collective-permute-done | bytes 1572896 | tf_op jit(solution)/shard_map/ppermute | solution.py:85
  204.7 3.0 fusion.101
  209.0 2.7 fusion.43
  215.8 4.2 fusion.112
  220.0 13.5 %concatenate.23 = f32[2,1664,384]{2,1,0:T(8,128)} concatenate(f32[2,1152,384]{2,1,0:T(8,128)} %bitcast.371, f32[2,384,384]{2,1,0:T(8,128)S(1)} %bitcast.389, f32[2,9,384]{2,1,0:T(8,128)S(1)} %copy-done.25, f32[2,119,384]{2,1,0:T(8,128)S(1)} %broadcast_in_dim.170), dimensions={1} | concatenate | bytes 10223616 | tf_op jit(solution)/shard_map/concatenate | solution.py:277
  233.4 3.4 dynamic-slice_bitcast_fusion.1
  236.8 3.1 collective-permute-start.4
  239.8 4.4 %bitcast_add_fusion = f32[1536,768]{1,0:T(8,128)S(1)} fusion(f32[1536,768]{1,0:T(8,128)} %collective-permute-done.19, f32[2,1536,768]{2,1,0:T(8,128)} %maximum_maximum_fusion, s32[]{:T(128)S(6)} %select_n.197), kind=kLoop, calls=%fused_computation.14 | loop fusion | flops 1179648 | bytes 14155780 | tf_op jit(solution)/shard_map/add | solution.py:72
  247.5 2.7 collective-permute-start.22
  251.2 25.1 %collective-permute-done.22 = f32[384,768]{1,0:T(8,128)S(1)} collective-permute-done((f32[384,768]{1,0:T(8,128)}, f32[384,768]{1,0:T(8,128)S(1)}, u32[]{:S(2)}, u32[]{:S(2)}) %collective-permute-start.22) | collective-permute-done | bytes 1179680 | tf_op jit(solution)/shard_map/ppermute | solution.py:55
  277.3 2.7 collective-permute-done.20
  293.0 8.0 %collective-permute-done.24 = f32[96,768]{1,0:T(8,128)S(1)} collective-permute-done((f32[96,768]{1,0:T(8,128)}, f32[96,768]{1,0:T(8,128)S(1)}, u32[]{:S(2)}, u32[]{:S(2)}) %collective-permute-start.24) | collective-permute-done | bytes 294944 | tf_op jit(solution)/shard_map/ppermute | solution.py:55
  301.0 11.0 %collective-permute-done.23 = f32[96,768]{1,0:T(8,128)} collective-permute-done((f32[96,768]{1,0:T(8,128)S(1)}, f32[96,768]{1,0:T(8,128)}, u32[]{:S(2)}, u32[]{:S(2)}) %collective-permute-start.23) | collective-permute-done | bytes 294944 | tf_op jit(solution)/shard_map/ppermute | solution.py:55
  318.8 3.1 collective-permute-done.26
  325.5 6.9 %collective-permute-done.27 = f32[96,768]{1,0:T(8,128)S(1)} collective-permute-done((f32[96,768]{1,0:T(8,128)S(1)}, f32[96,768]{1,0:T(8,128)S(1)}, u32[]{:S(2)}, u32[]{:S(2)}) %collective-permute-start.27) | collective-permute-done | bytes 294944 | tf_op jit(solution)/shard_map/ppermute | solution.py:64
  335.5 3.4 collective-permute-start.13
  338.9 2.6 broadcast_in_dim.182
  343.6 3.7 collective-permute-done.13
  348.8 17.0 %collective-permute-done.30 = f32[384,768]{1,0:T(8,128)} collective-permute-done((f32[384,768]{1,0:T(8,128)S(1)}, f32[384,768]{1,0:T(8,128)}, u32[]{:S(2)}, u32[]{:S(2)}) %collective-permute-start.30) | collective-permute-done | bytes 1179680 | tf_op jit(solution)/shard_map/ppermute | solution.py:64
  370.4 3.0 collective-permute-start.33
  377.0 7.4 %collective-permute-done.16 = f32[416,384]{1,0:T(8,128)S(1)} collective-permute-done((f32[416,384]{1,0:T(8,128)S(1)}, f32[416,384]{1,0:T(8,128)S(1)}, u32[]{:S(2)}, u32[]{:S(2)}) %collective-permute-start.16) | collective-permute-done | bytes 639008 | tf_op jit(solution)/shard_map/ppermute | solution.py:64
  384.5 5.2 %collective-permute-done.17 = f32[416,384]{1,0:T(8,128)S(1)} collective-permute-done((f32[416,384]{1,0:T(8,128)S(1)}, f32[416,384]{1,0:T(8,128)S(1)}, u32[]{:S(2)}, u32[]{:S(2)}) %collective-permute-start.17) | collective-permute-done | bytes 639008 | tf_op jit(solution)/shard_map/ppermute | solution.py:64
  390.4 4.3 %broadcast_in_dim.181 = f32[2,1536,768]{2,1,0:T(8,128)} broadcast(f32[]{:T(128)} %constant.328.clone.1), dimensions={} | broadcast | bytes 9437188 | tf_op jit(solution)/shard_map/broadcast_in_dim | solution.py:79
  394.7 4.8 %bitcast_dynamic-update-slice_fusion.1 = f32[2,1536,768]{2,1,0:T(8,128)} fusion(f32[2,1536,768]{2,1,0:T(8,128)} %broadcast_in_dim.181, s32[]{:T(128)S(6)} %select_n.197, f32[1,1536,768]{2,1,0:T(8,128)} %bitcast.356), kind=kLoop, calls=%fused_computation.13 | loop fusion | bytes 9437188 | tf_op jit(solution)/shard_map/jit(dynamic_update_index_in_dim)/dynamic_update_slice | solution.py:80
  405.5 4.0 copy.53
  413.3 4.8 %bitcast_dynamic-update-slice_fusion = f32[2,1536,768]{2,1,0:T(8,128)} fusion(f32[2,1536,768]{2,1,0:T(8,128)} %bitcast_dynamic-update-slice_fusion.1, s32[]{:T(128)S(6)} %select_n.198, f32[1536,768]{1,0:T(8,128)} %collective-permute-done.33), kind=kLoop, calls=%fused_computation.12 | loop fusion | bytes 9437188 | tf_op jit(solution)/shard_map/jit(dynamic_update_index_in_dim)/dynamic_update_slice | solution.py:81
  418.1 2.7 slice_bitcast_fusion.1
  420.8 4.8 %slice.94 = f32[2,768,768]{2,1,0:T(8,128)} slice(f32[2,1536,768]{2,1,0:T(8,128)} %bitcast_dynamic-update-slice_fusion), slice={[0:2], [0:768], [0:768]} | slice | bytes 9437184 | tf_op jit(solution)/shard_map/slice | solution.py:307
  425.6 2.9 pad_maximum_fusion
  (304 shorter events, 94.5 us)
Async XLA Ops:
  0.6 57.9 %copy-start = (bf16[768,1536]{1,0:T(8,128)(2,1)S(1)}, bf16[768,1536]{1,0:T(8,128)(2,1)}, u32[]{:S(2)}) copy-start(bf16[768,1536]{1,0:T(8,128)(2,1)} %param.25) | copy-start | bytes 7077892
  16.2 39.0 %collective-permute-start = (f32[512,768]{1,0:T(8,128)}, f32[512,768]{1,0:T(8,128)}, u32[]{:S(2)}, u32[]{:S(2)}) collective-permute-start(f32[512,768]{1,0:T(8,128)} %fusion.109), channel_id=1, source_target_pairs={{0,1},{1,0},{2,3},{3,2},{4,5},{5,4},{6,7},{7,6},{8,9},{9,8},{10,11... | collective-permute-start | bytes 4718600 | tf_op jit(solution)/shard_map/ppermute | solution.py:85
  24.4 49.5 %copy-start.37 = (f32[512]{0:T(512)}, f32[512]{0:T(512)S(1)}, u32[]{:S(2)}) copy-start(f32[512]{0:T(512)S(1)} %fusion.97) | copy-start | bytes 6148
  25.2 33.4 %copy-start.32 = (f32[768]{0:T(1024)S(1)}, f32[768]{0:T(1024)}, u32[]{:S(2)}) copy-start(f32[768]{0:T(1024)} %convert_element_type.151) | copy-start | bytes 9220
  25.2 33.4 %copy-start.58 = (f32[1536]{0:T(1024)S(1)}, f32[1536]{0:T(1024)}, u32[]{:S(2)}) copy-start(f32[1536]{0:T(1024)} %convert_element_type.154) | copy-start | bytes 18436
  25.2 33.3 %copy-start.64 = (f32[768]{0:T(1024)S(1)}, f32[768]{0:T(1024)}, u32[]{:S(2)}) copy-start(f32[768]{0:T(1024)} %convert_element_type.152) | copy-start | bytes 9220
  79.4 36.5 %collective-permute-start.2 = (f32[512,768]{1,0:T(8,128)}, f32[512,768]{1,0:T(8,128)}, u32[]{:S(2)}, u32[]{:S(2)}) collective-permute-start(f32[512,768]{1,0:T(8,128)} %fusion.110), channel_id=1, source_target_pairs={{0,1},{1,0},{2,3},{3,2},{4,5},{5,4},{6,7},{7,6},{8,9},{9,8},{10,11... | collective-permute-start | bytes 4718600 | tf_op jit(solution)/shard_map/ppermute | solution.py:85
  84.6 65.0 %collective-permute-start.1 = (f32[512,768]{1,0:T(8,128)}, f32[512,768]{1,0:T(8,128)}, u32[]{:S(2)}, u32[]{:S(2)}) collective-permute-start(f32[512,768]{1,0:T(8,128)} %fusion.54), channel_id=1, source_target_pairs={{0,1},{1,0},{2,3},{3,2},{4,5},{5,4},{6,7},{7,6},{8,9},{9,8},{10,11... | collective-permute-start | bytes 4718600 | tf_op jit(solution)/shard_map/ppermute | solution.py:85
  101.6 48.0 %copy-start.38 = (f32[512]{0:T(512)S(1)}, f32[512]{0:T(512)}, u32[]{:S(2)}) copy-start(f32[512]{0:T(512)} %copy-done.37) | copy-start | bytes 6148
  101.6 48.0 %copy-start.51 = (f32[768]{0:T(1024)S(1)}, f32[768]{0:T(1024)}, u32[]{:S(2)}) copy-start(f32[768]{0:T(1024)} %convert_element_type.156) | copy-start | bytes 9220
  169.1 35.6 %copy-start.28 = (f32[768]{0:T(1024)S(1)}, f32[768]{0:T(1024)}, u32[]{:S(2)}) copy-start(f32[768]{0:T(1024)} %copy-done.27) | copy-start | bytes 9220
  169.1 35.6 %copy-start.31 = (f32[512]{0:T(512)S(1)}, f32[512]{0:T(512)}, u32[]{:S(2)}) copy-start(f32[512]{0:T(512)} %copy-done.30) | copy-start | bytes 6148
  169.1 35.6 %collective-permute-start.3 = (f32[512,768]{1,0:T(8,128)}, f32[512,768]{1,0:T(8,128)}, u32[]{:S(2)}, u32[]{:S(2)}) collective-permute-start(f32[512,768]{1,0:T(8,128)} %fusion.111), channel_id=1, source_target_pairs={{0,1},{1,0},{2,3},{3,2},{4,5},{5,4},{6,7},{7,6},{8,9},{9,8},{10,11... | collective-permute-start | bytes 4718600 | tf_op jit(solution)/shard_map/ppermute | solution.py:85
  173.9 33.7 %copy-start.44 = (f32[512]{0:T(512)S(1)}, f32[512]{0:T(512)}, u32[]{:S(2)}) copy-start(f32[512]{0:T(512)} %copy-done.43) | copy-start | bytes 6148
  173.9 33.7 %copy-start.48 = (f32[512]{0:T(512)S(1)}, f32[512]{0:T(512)}, u32[]{:S(2)}) copy-start(f32[512]{0:T(512)} %copy-done.47) | copy-start | bytes 6148
  173.9 65.9 %collective-permute-start.19 = (f32[1536,768]{1,0:T(8,128)}, f32[1536,768]{1,0:T(8,128)}, u32[]{:S(2)}, u32[]{:S(2)}) collective-permute-start(f32[1536,768]{1,0:T(8,128)} %dynamic-slice_bitcast_fusion), channel_id=1, source_target_pairs={{0,2},{2,0},{4,6},{6,4},{8,10},{10,8},{12,14},{14,12},{16,18},{18,... | collective-permute-start | bytes 14155784 | tf_op jit(solution)/shard_map/ppermute | solution.py:72
  177.6 31.4 %copy-start.61 = (f32[512]{0:T(512)S(1)}, f32[512]{0:T(512)}, u32[]{:S(2)}) copy-start(f32[512]{0:T(512)} %copy-done.60) | copy-start | bytes 6148
  236.8 48.5 %collective-permute-start.4 = (f32[1664,384]{1,0:T(8,128)}, f32[1664,384]{1,0:T(8,128)}, u32[]{:S(2)}, u32[]{:S(2)}) collective-permute-start(f32[1664,384]{1,0:T(8,128)} %dynamic-slice_bitcast_fusion.1), channel_id=1, source_target_pairs={{0,2},{2,0},{4,6},{6,4},{8,10},{10,8},{12,14},{14,12},{16,18},{18,... | collective-permute-start | bytes 7667720 | tf_op jit(solution)/shard_map/ppermute | solution.py:72
  244.2 41.0 %slice-start.5 = ((s8[5111808]{0:T(1024)(128)(4,1)}), s8[917504]{0:T(1024)(128)(4,1)S(1)}, s32[]{:S(2)}) async-start(s8[5111808]{0:T(1024)(128)(4,1)} %bitcast.366), calls=%async_computation.5 | async-start | bytes 1835008
  247.5 28.8 %collective-permute-start.22 = (f32[384,768]{1,0:T(8,128)}, f32[384,768]{1,0:T(8,128)S(1)}, u32[]{:S(2)}, u32[]{:S(2)}) collective-permute-start(f32[384,768]{1,0:T(8,128)} %get-tuple-element.71), channel_id=1, source_target_pairs={{0,96},{2,14},{4,100},{6,2},{8,104},{10,6},{12,108},{14,10},{16,11... | collective-permute-start | bytes 3538952 | tf_op jit(solution)/shard_map/ppermute | solution.py:55
  250.2 26.1 %collective-permute-start.21 = (f32[384,768]{1,0:T(8,128)}, f32[384,768]{1,0:T(8,128)S(1)}, u32[]{:S(2)}, u32[]{:S(2)}) collective-permute-start(f32[384,768]{1,0:T(8,128)} %get-tuple-element.72), channel_id=1, source_target_pairs={{0,64},{2,10},{4,68},{6,14},{8,72},{10,2},{12,76},{14,6},{16,80},{... | collective-permute-start | bytes 3538952 | tf_op jit(solution)/shard_map/ppermute | solution.py:55
  250.5 29.4 %collective-permute-start.20 = (f32[384,768]{1,0:T(8,128)}, f32[384,768]{1,0:T(8,128)}, u32[]{:S(2)}, u32[]{:S(2)}) collective-permute-start(f32[384,768]{1,0:T(8,128)} %get-tuple-element.70), channel_id=1, source_target_pairs={{0,32},{2,6},{4,36},{6,10},{8,40},{10,14},{12,44},{14,2},{16,48},{... | collective-permute-start | bytes 3538952 | tf_op jit(solution)/shard_map/ppermute | solution.py:55
  251.2 34.0 %slice-start.6 = ((s8[5111808]{0:T(1024)(128)(4,1)}), s8[4194304]{0:T(1024)(128)(4,1)S(1)}, s32[]{:S(2)}) async-start(s8[5111808]{0:T(1024)(128)(4,1)} %bitcast.366), calls=%async_computation.6 | async-start | bytes 8388608
  283.0 8.7 %collective-permute-start.25 = (f32[96,768]{1,0:T(8,128)S(1)}, f32[96,768]{1,0:T(8,128)S(1)}, u32[]{:S(2)}, u32[]{:S(2)}) collective-permute-start(f32[96,768]{1,0:T(8,128)S(1)} %get-tuple-element.80), channel_id=1, source_target_pairs={{0,12},{2,98},{4,0},{6,102},{8,4},{10,106},{12,8},{14,110},{16,28}... | collective-permute-start | bytes 884744 | tf_op jit(solution)/shard_map/ppermute | solution.py:55
  289.7 23.8 %collective-permute-start.7 = (f32[416,384]{1,0:T(8,128)}, f32[416,384]{1,0:T(8,128)}, u32[]{:S(2)}, u32[]{:S(2)}) collective-permute-start(f32[416,384]{1,0:T(8,128)} %get-tuple-element.74), channel_id=1, source_target_pairs={{0,96},{2,14},{4,100},{6,2},{8,104},{10,6},{12,108},{14,10},{16,11... | collective-permute-start | bytes 1916936 | tf_op jit(solution)/shard_map/ppermute | solution.py:55
  290.6 22.9 %collective-permute-start.6 = (f32[416,384]{1,0:T(8,128)S(1)}, f32[416,384]{1,0:T(8,128)}, u32[]{:S(2)}, u32[]{:S(2)}) collective-permute-start(f32[416,384]{1,0:T(8,128)S(1)} %get-tuple-element.75), channel_id=1, source_target_pairs={{0,64},{2,10},{4,68},{6,14},{8,72},{10,2},{12,76},{14,6},{16,80},{... | collective-permute-start | bytes 1916936 | tf_op jit(solution)/shard_map/ppermute | solution.py:55
  290.7 24.2 %collective-permute-start.5 = (f32[416,384]{1,0:T(8,128)S(1)}, f32[416,384]{1,0:T(8,128)}, u32[]{:S(2)}, u32[]{:S(2)}) collective-permute-start(f32[416,384]{1,0:T(8,128)S(1)} %get-tuple-element.73), channel_id=1, source_target_pairs={{0,32},{2,6},{4,36},{6,10},{8,40},{10,14},{12,44},{14,2},{16,48},{... | collective-permute-start | bytes 1916936 | tf_op jit(solution)/shard_map/ppermute | solution.py:55
  291.2 9.8 %collective-permute-start.24 = (f32[96,768]{1,0:T(8,128)}, f32[96,768]{1,0:T(8,128)S(1)}, u32[]{:S(2)}, u32[]{:S(2)}) collective-permute-start(f32[96,768]{1,0:T(8,128)} %get-tuple-element.81), channel_id=1, source_target_pairs={{0,8},{2,66},{4,12},{6,70},{8,0},{10,74},{12,4},{14,78},{16,24},{1... | collective-permute-start | bytes 884744 | tf_op jit(solution)/shard_map/ppermute | solution.py:55
  292.4 19.5 %collective-permute-start.23 = (f32[96,768]{1,0:T(8,128)S(1)}, f32[96,768]{1,0:T(8,128)}, u32[]{:S(2)}, u32[]{:S(2)}) collective-permute-start(f32[96,768]{1,0:T(8,128)S(1)} %get-tuple-element.79), channel_id=1, source_target_pairs={{0,4},{2,34},{4,8},{6,38},{8,12},{10,42},{12,0},{14,46},{16,20},{1... | collective-permute-start | bytes 884744 | tf_op jit(solution)/shard_map/ppermute | solution.py:55
  313.1 8.9 %collective-permute-start.26 = (f32[96,768]{1,0:T(8,128)S(1)}, f32[96,768]{1,0:T(8,128)S(1)}, u32[]{:S(2)}, u32[]{:S(2)}) collective-permute-start(f32[96,768]{1,0:T(8,128)S(1)} %fusion.91), channel_id=1, source_target_pairs={{0,16},{2,18},{4,20},{6,22},{8,24},{10,26},{12,28},{14,30},{16,0},... | collective-permute-start | bytes 884744 | tf_op jit(solution)/shard_map/ppermute | solution.py:75
  317.4 5.4 %collective-permute-start.10 = (f32[104,384]{1,0:T(8,128)}, f32[104,384]{1,0:T(8,128)S(1)}, u32[]{:S(2)}, u32[]{:S(2)}) collective-permute-start(f32[104,384]{1,0:T(8,128)} %get-tuple-element.84), channel_id=1, source_target_pairs={{0,12},{2,98},{4,0},{6,102},{8,4},{10,106},{12,8},{14,110},{16,28}... | collective-permute-start | bytes 479240 | tf_op jit(solution)/shard_map/ppermute | solution.py:55
  317.4 7.6 %collective-permute-start.9 = (f32[104,384]{1,0:T(8,128)S(1)}, f32[104,384]{1,0:T(8,128)S(1)}, u32[]{:S(2)}, u32[]{:S(2)}) collective-permute-start(f32[104,384]{1,0:T(8,128)S(1)} %get-tuple-element.85), channel_id=1, source_target_pairs={{0,8},{2,66},{4,12},{6,70},{8,0},{10,74},{12,4},{14,78},{16,24},{1... | collective-permute-start | bytes 479240 | tf_op jit(solution)/shard_map/ppermute | solution.py:55
  318.0 7.0 %collective-permute-start.8 = (f32[104,384]{1,0:T(8,128)S(1)}, f32[104,384]{1,0:T(8,128)S(1)}, u32[]{:S(2)}, u32[]{:S(2)}) collective-permute-start(f32[104,384]{1,0:T(8,128)S(1)} %get-tuple-element.83), channel_id=1, source_target_pairs={{0,4},{2,34},{4,8},{6,38},{8,12},{10,42},{12,0},{14,46},{16,20},{1... | collective-permute-start | bytes 479240 | tf_op jit(solution)/shard_map/ppermute | solution.py:55
  322.1 10.3 %collective-permute-start.27 = (f32[96,768]{1,0:T(8,128)S(1)}, f32[96,768]{1,0:T(8,128)S(1)}, u32[]{:S(2)}, u32[]{:S(2)}) collective-permute-start(f32[96,768]{1,0:T(8,128)S(1)} %get-tuple-element.57), channel_id=1, source_target_pairs={{0,4},{2,34},{4,8},{6,38},{8,12},{10,42},{12,0},{14,46},{16,20},{1... | collective-permute-start | bytes 884744 | tf_op jit(solution)/shard_map/ppermute | solution.py:64
  322.2 10.2 %collective-permute-start.28 = (f32[96,768]{1,0:T(8,128)S(1)}, f32[96,768]{1,0:T(8,128)S(1)}, u32[]{:S(2)}, u32[]{:S(2)}) collective-permute-start(f32[96,768]{1,0:T(8,128)S(1)} %get-tuple-element.57), channel_id=1, source_target_pairs={{0,8},{2,66},{4,12},{6,70},{8,0},{10,74},{12,4},{14,78},{16,24},{1... | collective-permute-start | bytes 884744 | tf_op jit(solution)/shard_map/ppermute | solution.py:64
  322.8 10.2 %collective-permute-start.29 = (f32[96,768]{1,0:T(8,128)S(1)}, f32[96,768]{1,0:T(8,128)S(1)}, u32[]{:S(2)}, u32[]{:S(2)}) collective-permute-start(f32[96,768]{1,0:T(8,128)S(1)} %get-tuple-element.57), channel_id=1, source_target_pairs={{0,12},{2,98},{4,0},{6,102},{8,4},{10,106},{12,8},{14,110},{16,28}... | collective-permute-start | bytes 884744 | tf_op jit(solution)/shard_map/ppermute | solution.py:64
  325.1 9.7 %collective-permute-start.11 = (f32[104,384]{1,0:T(8,128)S(1)}, f32[104,384]{1,0:T(8,128)S(1)}, u32[]{:S(2)}, u32[]{:S(2)}) collective-permute-start(f32[104,384]{1,0:T(8,128)S(1)} %fusion.93), channel_id=1, source_target_pairs={{0,16},{2,18},{4,20},{6,22},{8,24},{10,26},{12,28},{14,30},{16,0},... | collective-permute-start | bytes 479240 | tf_op jit(solution)/shard_map/ppermute | solution.py:75
  333.0 32.8 %collective-permute-start.30 = (f32[384,768]{1,0:T(8,128)S(1)}, f32[384,768]{1,0:T(8,128)}, u32[]{:S(2)}, u32[]{:S(2)}) collective-permute-start(f32[384,768]{1,0:T(8,128)S(1)} %bitcast.380), channel_id=1, source_target_pairs={{0,32},{2,6},{4,36},{6,10},{8,40},{10,14},{12,44},{14,2},{16,48},{... | collective-permute-start | bytes 3538952 | tf_op jit(solution)/shard_map/ppermute | solution.py:64
  333.1 35.1 %collective-permute-start.31 = (f32[384,768]{1,0:T(8,128)S(1)}, f32[384,768]{1,0:T(8,128)S(1)}, u32[]{:S(2)}, u32[]{:S(2)}) collective-permute-start(f32[384,768]{1,0:T(8,128)S(1)} %bitcast.381), channel_id=1, source_target_pairs={{0,64},{2,10},{4,68},{6,14},{8,72},{10,2},{12,76},{14,6},{16,80},{... | collective-permute-start | bytes 3538952 | tf_op jit(solution)/shard_map/ppermute | solution.py:64
  335.5 7.5 %collective-permute-start.12 = (f32[104,384]{1,0:T(8,128)}, f32[104,384]{1,0:T(8,128)S(1)}, u32[]{:S(2)}, u32[]{:S(2)}) collective-permute-start(f32[104,384]{1,0:T(8,128)} %get-tuple-element.59), channel_id=1, source_target_pairs={{0,4},{2,34},{4,8},{6,38},{8,12},{10,42},{12,0},{14,46},{16,20},{1... | collective-permute-start | bytes 479240 | tf_op jit(solution)/shard_map/ppermute | solution.py:64
  335.5 11.8 %collective-permute-start.13 = (f32[104,384]{1,0:T(8,128)}, f32[104,384]{1,0:T(8,128)S(1)}, u32[]{:S(2)}, u32[]{:S(2)}) collective-permute-start(f32[104,384]{1,0:T(8,128)} %get-tuple-element.59), channel_id=1, source_target_pairs={{0,8},{2,66},{4,12},{6,70},{8,0},{10,74},{12,4},{14,78},{16,24},{1... | collective-permute-start | bytes 479240 | tf_op jit(solution)/shard_map/ppermute | solution.py:64
  338.9 8.4 %collective-permute-start.14 = (f32[104,384]{1,0:T(8,128)}, f32[104,384]{1,0:T(8,128)S(1)}, u32[]{:S(2)}, u32[]{:S(2)}) collective-permute-start(f32[104,384]{1,0:T(8,128)} %get-tuple-element.59), channel_id=1, source_target_pairs={{0,12},{2,98},{4,0},{6,102},{8,4},{10,106},{12,8},{14,110},{16,28}... | collective-permute-start | bytes 479240 | tf_op jit(solution)/shard_map/ppermute | solution.py:64
  343.0 26.3 %collective-permute-start.32 = (f32[384,768]{1,0:T(8,128)S(1)}, f32[384,768]{1,0:T(8,128)S(1)}, u32[]{:S(2)}, u32[]{:S(2)}) collective-permute-start(f32[384,768]{1,0:T(8,128)S(1)} %bitcast.383), channel_id=1, source_target_pairs={{0,96},{2,14},{4,100},{6,2},{8,104},{10,6},{12,108},{14,10},{16,11... | collective-permute-start | bytes 3538952 | tf_op jit(solution)/shard_map/ppermute | solution.py:64
  347.3 29.6 %collective-permute-start.15 = (f32[416,384]{1,0:T(8,128)S(1)}, f32[416,384]{1,0:T(8,128)S(1)}, u32[]{:S(2)}, u32[]{:S(2)}) collective-permute-start(f32[416,384]{1,0:T(8,128)S(1)} %bitcast.398), channel_id=1, source_target_pairs={{0,32},{2,6},{4,36},{6,10},{8,40},{10,14},{12,44},{14,2},{16,48},{... | collective-permute-start | bytes 1916936 | tf_op jit(solution)/shard_map/ppermute | solution.py:64
  370.4 42.9 %collective-permute-start.33 = (f32[1536,768]{1,0:T(8,128)}, f32[1536,768]{1,0:T(8,128)}, u32[]{:S(2)}, u32[]{:S(2)}) collective-permute-start(f32[1536,768]{1,0:T(8,128)} %bitcast.101), channel_id=1, source_target_pairs={{0,2},{2,0},{4,6},{6,4},{8,10},{10,8},{12,14},{14,12},{16,18},{18,... | collective-permute-start | bytes 14155784 | tf_op jit(solution)/shard_map/ppermute | solution.py:78
  373.3 11.1 %collective-permute-start.16 = (f32[416,384]{1,0:T(8,128)S(1)}, f32[416,384]{1,0:T(8,128)S(1)}, u32[]{:S(2)}, u32[]{:S(2)}) collective-permute-start(f32[416,384]{1,0:T(8,128)S(1)} %bitcast.399), channel_id=1, source_target_pairs={{0,64},{2,10},{4,68},{6,14},{8,72},{10,2},{12,76},{14,6},{16,80},{... | collective-permute-start | bytes 1916936 | tf_op jit(solution)/shard_map/ppermute | solution.py:64
  374.8 14.9 %collective-permute-start.17 = (f32[416,384]{1,0:T(8,128)S(1)}, f32[416,384]{1,0:T(8,128)S(1)}, u32[]{:S(2)}, u32[]{:S(2)}) collective-permute-start(f32[416,384]{1,0:T(8,128)S(1)} %bitcast.400), channel_id=1, source_target_pairs={{0,96},{2,14},{4,100},{6,2},{8,104},{10,6},{12,108},{14,10},{16,11... | collective-permute-start | bytes 1916936 | tf_op jit(solution)/shard_map/ppermute | solution.py:64
  389.7 9.8 %collective-permute-start.18 = (f32[1664,384]{1,0:T(8,128)S(1)}, f32[1664,384]{1,0:T(8,128)S(1)}, u32[]{:S(2)}, u32[]{:S(2)}) collective-permute-start(f32[1664,384]{1,0:T(8,128)S(1)} %bitcast.376), channel_id=1, source_target_pairs={{0,2},{2,0},{4,6},{6,4},{8,10},{10,8},{12,14},{14,12},{16,18},{18,... | collective-permute-start | bytes 7667720 | tf_op jit(solution)/shard_map/ppermute | solution.py:78
  (63 other events, 523.0 us)
